TPU v7x, 32 devices: a whole 2x2x4 slice. The times are simulated.
32 devices in a mesh: groups: 2 (over y), replica: 4 (over z), tensor: 4 (over x, core).
Axes of the slice: x: 2, y: 2, z: 4, core: 2. Of those that a mesh axis runs over, the one named last changes fastest.
Arguments:
- queries: bfloat16 [512, 64, 128], P(('groups', 'replica'), 'tensor'), parts along dimension 0, may hold values from -256 to 256
- prefix_pool: bfloat16 [16, 64, 2, 8, 128], P(('groups', 'replica'), None, None, 'tensor'), parts along dimension 0, may hold values from -8 to 8
- page_table: int32 [12], P('groups'), parts along dimension 0, may hold values from 0 to 7, as said below
- suffix_kv: bfloat16 [512, 24, 2, 8, 128], P(('groups', 'replica'), None, None, 'tensor'), parts along dimension 0, may hold values from -9 to 9
- new_kv: bfloat16 [512, 2, 8, 128], P(('groups', 'replica'), None, 'tensor'), parts along dimension 0, may hold values from -10 to 10
- suffix_len: int32 [512], P(('groups', 'replica')), parts along dimension 0, may hold values from 0 to 24
- counts: int32 [8], P(('groups', 'replica')), parts along dimension 0, may hold values from 0 to 64, as said below
Outputs:
- attended: bfloat16 [512, 64, 128], P(('groups', 'replica'), 'tensor'), parts along dimension 0
There are 2 independent parts, one for each index of `groups`. A program takes and returns all parts, laid end to end along the dimension named above; each array names one. Nothing has to cross between parts.
Inputs may be any that keep to these rules, and one draw needn't show every extreme that they name: `page_table`: 6 distinct pool slots, among them slots 0 and 7. The counts of replicas 2i and 2i + 1 sum to 64.
All inputs are finite; a program needn't handle non-finite values.
Results may differ from a plain program's by a relative error of at most 0.013.
Values may be sent and summed in bfloat16 or wider, within the bound.
No kernel may reach another device: no remote copies, remote signals or barrier semaphores. Data moves between devices by JAX's collectives and lax.ppermute only.
A program may use at most 64 MiB of HBM per device.

v0:
```python
import math

import jax
import jax.numpy as jnp
from jax import lax
from jax.sharding import PartitionSpec as P

masked_score = -1e30


def empty_part(grouped):
    stat_shape = grouped.shape[:3]
    return (
        jnp.full(stat_shape, masked_score, jnp.float32),
        jnp.zeros(stat_shape, jnp.float32),
        jnp.zeros(grouped.shape, jnp.float32),
    )


def absorb(running, scores, contract):
    row_max = jnp.maximum(running[0], jnp.max(scores, axis=-1))
    factor = jnp.exp(running[0] - row_max)
    weights = jnp.exp(scores - row_max[..., None])
    row_total = running[1] * factor + jnp.sum(weights, axis=-1)
    accumulated = running[2] * factor[..., None] + contract(weights.astype(jnp.bfloat16))
    return (row_max, row_total, accumulated)


def merge_parts(earlier, later):
    row_max = jnp.maximum(earlier[0], later[0])
    scale_a = jnp.exp(earlier[0] - row_max)
    scale_b = jnp.exp(later[0] - row_max)
    row_total = earlier[1] * scale_a + later[1] * scale_b
    accumulated = earlier[2] * scale_a[..., None] + later[2] * scale_b[..., None]
    return (row_max, row_total, accumulated)


def fold_pages(running, grouped, piece, page_table):
    page_size = piece.shape[1]
    factor_q = grouped.shape[-1] ** (-0.5)
    slot_total = piece.shape[0]
    key_target = max(page_size, 32768 // grouped.shape[0])
    slot_block = math.gcd(slot_total, max(1, key_target // page_size))
    slot_ids = jnp.arange(slot_total, dtype=jnp.int32)
    live_slots = jnp.any(page_table[None, :] == slot_ids[:, None], axis=1)
    blocks = piece.reshape((slot_total // slot_block, slot_block * page_size) + piece.shape[2:])
    key_masks = jnp.repeat(
        live_slots.reshape(slot_total // slot_block, slot_block), page_size, axis=1
    )

    def absorb_block(inner_running, block_item):
        block, key_mask = block_item
        scores = (
            jnp.einsum("rgqd,kgd->rgqk", grouped, block[:, 0], preferred_element_type=jnp.float32)
            * factor_q
        )
        scores = jnp.where(key_mask[None, None, None, :], scores, masked_score)

        def contract(weights):
            return jnp.einsum(
                "rgqk,kgd->rgqd", weights, block[:, 1], preferred_element_type=jnp.float32
            )

        return (absorb(inner_running, scores, contract), None)

    result, unused = lax.scan(absorb_block, running, (blocks, key_masks))
    return result


def prefix_rows(grouped, prefix_pool, page_table):
    return fold_pages(
        empty_part(grouped),
        grouped,
        lax.all_gather(prefix_pool, "replica", axis=0, tiled=True),
        page_table,
    )


def suffix_part(grouped, suffix_kv, new_kv, suffix_len):
    factor_q = grouped.shape[-1] ** (-0.5)
    scores = (
        jnp.einsum(
            "rgqd,rkgd->rgqk", grouped, suffix_kv[:, :, 0], preferred_element_type=jnp.float32
        )
        * factor_q
    )
    kept_keys = jnp.arange(suffix_kv.shape[1], dtype=jnp.int32)[None, :] < suffix_len[:, None]
    scores = jnp.where(kept_keys[:, None, None, :], scores, masked_score)

    def contract_suffix(weights):
        return jnp.einsum(
            "rgqk,rkgd->rgqd", weights, suffix_kv[:, :, 1], preferred_element_type=jnp.float32
        )

    running = absorb(empty_part(grouped), scores, contract_suffix)
    fresh_score = (
        jnp.einsum("rgqd,rgd->rgq", grouped, new_kv[:, 0], preferred_element_type=jnp.float32)
        * factor_q
    )

    def contract_new(weights):
        return jnp.einsum(
            "rgqk,rgd->rgqd", weights, new_kv[:, 1], preferred_element_type=jnp.float32
        )

    return absorb(running, fresh_score[..., None], contract_new)


def shards(queries, prefix_pool, page_table, suffix_kv, new_kv, suffix_len, counts):
    slot_rows = queries.shape[0]
    head_count = queries.shape[1]
    kv_heads = prefix_pool.shape[3]
    grouped = queries.reshape(slot_rows, kv_heads, head_count // kv_heads, queries.shape[2])
    slot_count = counts[0]
    prefix = prefix_rows(grouped, prefix_pool, page_table)
    combined = merge_parts(prefix, suffix_part(grouped, suffix_kv, new_kv, suffix_len))
    result = combined[2] / combined[1][..., None]
    live_rows = jnp.arange(slot_rows, dtype=jnp.int32) < slot_count
    result = jnp.where(live_rows[:, None, None, None], result, 0.0)
    return result.reshape(slot_rows, head_count, queries.shape[2]).astype(jnp.bfloat16)


def solution(mesh):
    placed = (
        P(("groups", "replica"), "tensor", None),
        P(("groups", "replica"), None, None, "tensor", None),
        P("groups"),
        P(("groups", "replica"), None, None, "tensor", None),
        P(("groups", "replica"), None, "tensor", None),
        P(("groups", "replica")),
        P(("groups", "replica")),
    )
    return jax.shard_map(
        shards,
        mesh=mesh,
        in_specs=placed,
        out_specs=P(("groups", "replica"), "tensor", None),
        check_vma=False,
    )
```

profile of v0, /device:TPU:0, one launch (start us, length us, event | category | flops | bytes accessed | tf_op | source)
XLA Modules:
  0.0 32.0 jit_solution(2898645343890755833)
XLA Ops:
  0.0 0.0 copy-start
  0.0 1.0 %copy.75 = bf16[2,64,2,2,128]{4,1,3,2,0:T(8,128)(2,1)S(1)} copy(bf16[2,64,2,2,128]{4,3,2,1,0:T(2,128)(2,1)} %param.8) | data formatting | bytes 262144 | tf_op args[1]
  1.0 17.4 %all_gather.3 = bf16[8,64,2,2,128]{4,1,3,2,0:T(8,128)(2,1)S(1)} all-gather(bf16[2,64,2,2,128]{4,1,3,2,0:T(8,128)(2,1)S(1)} %copy.75), channel_id=1, replica_groups=mesh['groups'=2,'replica'=4,'tensor'=4] {'replica'}, dimensions={0}, use_global_device_ids=true | all-gather | bytes 655360 | tf_op jit(solution)/shard_map/all_gather | solution.py:74
  18.4 0.8 %fusion.26 = pred[8]{0:T(512)(128)(4,1)S(1)} fusion(s32[6]{0:T(128)} %param.9), kind=kLoop, calls=%fused_computation.52 | loop fusion | flops 88 | bytes 32 | tf_op jit(solution)/shard_map/reduce_or | solution.py:45
  19.1 0.1 broadcast_in_dim.64
  19.2 0.1 broadcast_in_dim.65
  19.3 0.0 copy-done
  19.3 0.5 %bitcast_reduce_fusion = (f32[64,2,8]{0,2,1:T(8,128)S(1)}, f32[2,512,64,8]{1,2,3,0:T(8,128)S(1)}) fusion(pred[512]{0:T(512)(128)(4,1)S(1)} %broadcast_in_dim.65, bf16[64,2,8,128]{3,2,1,0:T(8,128)(2,1)S(1)} %bitcast.91, bf16[512,2,2,128]{3,0,2,1:T(8,128)(2,1)S(1)} %bitcast.92), kind=kOutput, calls=%fused_computation.1 | convolution fusion | flops 135789568 | bytes 2626048 | tf_op jit(solution)/shard_map/while/body/eval_jaxpr/rgqd,kgd->rgqk/dot_general | solution.py:54
  19.8 0.0 copy-start.1
  19.9 1.3 %fusion.1 = (f32[64,2,8]{0,2,1:T(8,128)}, bf16[64,2,8,512]{3,0,2,1:T(8,128)(2,1)S(1)}) fusion(f32[2,512,64,8]{1,2,3,0:T(8,128)S(1)} %get-tuple-element.44, f32[64,2,8]{0,2,1:T(8,128)S(1)} %broadcast_maximum_fusion.1, pred[512]{0:T(512)(128)(4,1)S(1)} %broadcast_in_dim.65), kind=kLoop, calls=%fused_computation.4 | loop fusion | flops 2620416 | bytes 3154432 | tf_op jit(solution)/shard_map/while/body/eval_jaxpr/reduce_sum | solution.py:24
  21.1 0.0 copy-start.2
  21.1 0.1 copy-done.1
  21.3 1.1 %fusion.29 = (bf16[64,24,1,2,128]{4,3,2,1,0:T(2,128)(2,1)S(1)}, bf16[64,24,1,2,128]{4,3,2,1,0:T(2,128)(2,1)S(1)}) fusion(bf16[64,24,2,2,128]{4,3,2,1,0:T(2,128)(2,1)S(1)} %copy-done.1), kind=kLoop, calls=%fused_computation.56 | loop fusion | bytes 3145728 | tf_op jit(solution)/shard_map/slice | solution.py:83
  22.3 0.0 copy-done.2
  22.3 0.1 iota_compare_fusion
  22.4 0.7 %fusion.30 = (f32[64,2,8]{2,1,0:T(2,128)S(1)}, f32[64,2,8,24]{3,2,1,0:T(8,128)S(1)}) fusion(bf16[64,24,1,2,128]{4,3,2,1,0:T(2,128)(2,1)S(1)} %get-tuple-element.19, bf16[64,16,128]{2,1,0:T(8,128)(2,1)S(1)} %copy-done, pred[64,24]{1,0:T(8,128)(4,1)S(1)} %iota_compare_fusion), kind=kOutput, calls=%fused_computation.57 | convolution fusion | flops 6364160 | bytes 1152512 | tf_op jit(solution)/shard_map/rgqd,rkgd->rgqk/dot_general | solution.py:82
  23.1 0.1 copy.81
  23.2 0.1 copy.84
  23.3 0.4 %fusion.16 = (f32[64,2,8]{2,1,0:T(2,128)S(1)}, bf16[64,2,8,24]{3,2,1,0:T(8,128)(2,1)S(1)}) fusion(f32[64,2,8,24]{3,2,1,0:T(8,128)S(1)} %get-tuple-element.42, f32[64,2,8]{2,1,0:T(2,128)S(1)} %copy.84), kind=kLoop, calls=%fused_computation.24 | loop fusion | flops 72704 | bytes 155648 | tf_op jit(solution)/shard_map/reduce_sum | solution.py:24
  23.8 0.1 copy.91
  23.8 0.8 %bitcast_convert_fusion = (f32[64,2,128]{2,1,0:T(2,128)S(1)}, bf16[64,2,128,1]{2,1,0,3:T(2,128)(2,1)S(1)}) fusion(bf16[64,2,2,128]{3,2,1,0:T(2,128)(2,1)} %param.11), kind=kLoop, calls=%fused_computation.34 | loop fusion | flops 16384 | bytes 163840 | tf_op jit(solution)/shard_map/convert.3
  24.7 0.3 fusion.21
  24.9 0.1 copy.97
  25.0 0.7 %fusion.23 = (f32[64,2,8]{0,2,1:T(8,128)S(1)}, f32[64,2,8]{0,2,1:T(8,128)S(1)}, f32[64,2,8]{0,2,1:T(8,128)S(1)}, f32[64,2,8]{0,2,1:T(8,128)S(1)}, f32[64,2,8]{0,...) fusion(f32[64,2,1,8]{0,3,1,2:T(8,128)S(1)} %copy.97, f32[64,2,8]{0,2,1:T(8,128)S(1)} %get-tuple-element.43, ...), kind=kLoop, calls=%fused_computation.39 | loop fusion | flops 22528 | bytes 49152 | tf_op jit(solution)/shard_map/exp | solution.py:31
  25.7 0.1 copy.83
  25.8 0.1 copy.87
  25.9 0.1 copy.88
  26.0 0.1 copy.90
  26.2 1.5 %fusion.11 = f32[64,2,8,128]{3,2,0,1:T(8,128)} fusion(bf16[64,24,1,2,128]{4,3,2,1,0:T(2,128)(2,1)S(1)} %get-tuple-element.20, bf16[64,2,8,24]{3,2,1,0:T(8,128)(2,1)S(1)} %get-tuple-element.30, f32[64,2,8]{2,0,1:T(8,128)S(1)} %copy.90, f32[64,2,128]{2,0,1:T(8,128)S(1)} %copy.89, f32[64,2,8]{2,0,1:T(8,128)S(1)} %copy.88, f32[64,2,8]{2,0,1:T(8,128)S(1)} %copy.87, ...), kind=kOutput, calls=%fused_computation.17 | convolution fusion | flops 6946816 | bytes 1441792 | tf_op jit(solution)/shard_map/rgqk,rkgd->rgqd/dot_general | solution.py:91
  27.7 0.1 copy.78
  27.8 0.1 copy.82
  27.9 0.1 copy.92
  28.6 2.7 %fusion.12 = bf16[64,2,8,128]{3,2,0,1:T(8,128)(2,1)S(1)} fusion(f32[64,2,8,128]{3,2,0,1:T(8,128)} %fusion.11, bf16[64,2,8,512]{3,0,2,1:T(8,128)(2,1)S(1)} %get-tuple-element.18, bf16[512,2,2,128]{3,0,2,1:T(8,128)(2,1)S(1)} %bitcast.93, f32[64,2,8]{2,0,1:T(8,128)S(1)} %copy.92, f32[64,2,8]{2,0,1:T(8,128)S(1)} %copy.82, f32[64,2,8]{2,0,1:T(8,128)S(1)} %copy.78, ...), kind=kOutput, calls=%fused_computation.18 | convolution fusion | flops 135004160 | bytes 2294272 | tf_op jit(solution)/shard_map/while/body/eval_jaxpr/rgqk,kgd->rgqd/dot_general | solution.py:60
  31.3 0.7 %copy.123 = bf16[64,2,8,128]{3,2,1,0:T(8,128)(2,1)} copy(bf16[64,2,8,128]{3,2,0,1:T(8,128)(2,1)S(1)} %fusion.12) | data formatting | bytes 524288 | tf_op jit(solution)/shard_map/convert_element_type | solution.py:120
  (5 shorter events, 0.1 us)
Async XLA Ops:
  0.0 19.3 %copy-start = (bf16[64,16,128]{2,1,0:T(8,128)(2,1)S(1)}, bf16[64,16,128]{2,1,0:T(8,128)(2,1)}, u32[]{:S(2)}) copy-start(bf16[64,16,128]{2,1,0:T(8,128)(2,1)} %param.7) | copy-start | bytes 786436
  19.8 1.4 %copy-start.1 = (bf16[64,24,2,2,128]{4,3,2,1,0:T(2,128)(2,1)S(1)}, bf16[64,24,2,2,128]{4,3,2,1,0:T(2,128)(2,1)}, u32[]{:S(2)}) copy-start(bf16[64,24,2,2,128]{4,3,2,1,0:T(2,128)(2,1)} %param.10) | copy-start | bytes 4718596
  21.1 1.2 %copy-start.2 = (s32[64]{0:T(128)S(1)}, s32[64]{0:T(128)}, u32[]{:S(2)}) copy-start(s32[64]{0:T(128)} %param.12) | copy-start | bytes 772
where the time goes:
time: 32.4 us; the launch traced here: 32 us
  blocking collectives  17.4 us (54%)
  matrix products  5.68 us (18%)
  local copies, waits for them, and re-layouts  4.11 us (13%)
  other arithmetic  4.1 us (13%)
  between operations  0.81 us (2%)
    all_gather x1, blocking collectives, prefix_rows(): lax.all_gather(prefix_pool, 'replica', axis=0, tiled=True)  17.4 us
    dot_general x1, matrix products, contract(): jnp.einsum('rgqk,kgd->rgqd', weights, block[:, 1], preferred_element_type...  2.66 us
    reduce_sum x2, other arithmetic, absorb(): row_total = running[1] * factor + jnp.sum(weights, axis=-1)  1.67 us
    dot_general x1, matrix products, contract_suffix(): jnp.einsum('rgqk,rkgd->rgqd', weights, suffix_kv[:, :, 1], preferred_elem...  1.51 us
    unnamed x7, local copies, waits for them, and re-layouts  1.11 us
    slice x1, local copies, waits for them, and re-layouts, suffix_part(): suffix_kv[:, :, 0]  1.08 us
    another operation x1, other arithmetic  0.83 us
    reduce_or x1, other arithmetic, fold_pages(): live_slots = jnp.any(page_table[None, :] == slot_ids[:, None], axis=1)  0.77 us

commit v1 on v0

v1 whole, which is shorter than its diff:
```python
import functools
import math

import jax
import jax.numpy as jnp
from jax import lax
from jax.experimental import pallas as pl
from jax.experimental.pallas import tpu as pltpu
from jax.sharding import PartitionSpec as P

masked_score = -1e30
lanes = 128


def one_hot(shape, condition):
    row = lax.broadcasted_iota(jnp.int32, shape, 0)
    column = lax.broadcasted_iota(jnp.int32, shape, 1)
    return jnp.where(condition(row, column), 1.0, 0.0).astype(jnp.bfloat16)


def head_concat(grouped, heads, group):
    row = lax.broadcasted_iota(jnp.int32, grouped.shape, 0)
    head = lax.rem(row, heads * group) // group
    values = grouped.astype(jnp.float32)
    parts = [jnp.where(head == g, values, 0.0).astype(jnp.bfloat16) for g in range(heads)]
    return jnp.concatenate(parts, axis=1)


def head_select(wide, heads, group):
    width = wide.shape[1] // heads
    shape = (wide.shape[0], width)
    head = lax.rem(lax.broadcasted_iota(jnp.int32, shape, 0), heads * group) // group
    result = wide[:, :width]
    for g in range(1, heads):
        result = jnp.where(head == g, wide[:, g * width : (g + 1) * width], result)
    return result


def split_page(raw, order, heads):
    sorted_rows = jnp.dot(order, raw, preferred_element_type=jnp.float32).astype(jnp.bfloat16)
    tokens = raw.shape[0] // (2 * heads)
    kinds = [sorted_rows[i * tokens : (i + 1) * tokens] for i in range(2 * heads)]
    return jnp.concatenate(kinds[:heads], axis=1), jnp.concatenate(kinds[heads:], axis=1)


def page_order(page_rows, kinds):
    tokens = page_rows // kinds
    return one_hot(
        (page_rows, page_rows),
        lambda row, column: column == lax.rem(row, tokens) * kinds + row // tokens,
    )


def slot_live(table_ref, slot):
    found = jnp.int32(0)
    for index in range(table_ref.shape[0]):
        found = jnp.maximum(found, (table_ref[index] == slot).astype(jnp.int32))
    return found


def live_lanes(table_ref, slots, page):
    column = lax.broadcasted_iota(jnp.int32, (1, len(slots) * page), 1)
    live = jnp.zeros_like(column)
    for place, slot in enumerate(slots):
        live = jnp.where(column // page == place, slot_live(table_ref, slot), live)
    return live


def fill_tables(raws, order, keys_ref, values_ref, heads, page):
    place = 0
    page_rows = page * 2 * heads
    for raw_ref in raws:
        for at in range(0, raw_ref.shape[0], page_rows):
            keys, values = split_page(raw_ref[at : at + page_rows], order, heads)
            keys_ref[place : place + page] = keys
            values_ref[place : place + page] = values
            place += page


def contract_last(a, b):
    return lax.dot_general(a, b, (((1,), (1,)), ((), ())), preferred_element_type=jnp.float32)


def local_body(
    sizes, table_ref, lens_ref, q_ref, own_ref, suffix_ref, new_ref, acc_ref, stat_ref, keys_ref, values_ref
):
    heads, group, page, suffix, scale, batch = sizes
    kinds = 2 * heads
    row_heads = heads * group
    me = lax.axis_index("replica")
    slots = own_ref.shape[0] // (page * kinds)
    fill_tables([own_ref], page_order(page * kinds, kinds), keys_ref, values_ref, heads, page)
    live = live_lanes(table_ref, [me * slots + s for s in range(slots)], page)
    cached = suffix * kinds
    fresh = batch * kinds
    width = cached + fresh
    column = lax.broadcasted_iota(jnp.int32, (row_heads, width), 1)
    head = lax.broadcasted_iota(jnp.int32, (row_heads, width), 0) // group
    never = jnp.int32(1 << 20)
    token = jnp.where(
        (column < cached) & (lax.rem(column, kinds) == head), column // kinds, never
    )
    block_rows = batch * row_heads
    keys = keys_ref[...]
    values = values_ref[...]

    def one_block(step, carry):
        rows = pl.ds(pl.multiple_of(step * block_rows, block_rows), block_rows)
        q = q_ref[rows]
        prefix = contract_last(head_concat(q, heads, group), keys) * scale
        prefix = jnp.where(live > 0, prefix, masked_score)
        new_rows = new_ref[pl.ds(pl.multiple_of(step * fresh, fresh), fresh)]
        own_kv = []
        scores = []
        for i in range(batch):
            at = pl.multiple_of((step * batch + i) * cached, cached)
            kv = jnp.concatenate([suffix_ref[pl.ds(at, cached)], new_rows], axis=0)
            own_kv.append(kv)
            place = jnp.where(column == cached + i * kinds + head, -1, token)
            score = contract_last(q[i * row_heads : (i + 1) * row_heads], kv) * scale
            scores.append(jnp.where(place < lens_ref[step * batch + i], score, masked_score))
        score = jnp.concatenate(scores, axis=0)
        row_max = jnp.maximum(
            jnp.max(prefix, axis=1, keepdims=True), jnp.max(score, axis=1, keepdims=True)
        )
        weights = jnp.exp2(score - row_max)
        prefix_weights = jnp.exp2(prefix - row_max)
        total = jnp.sum(weights, axis=1, keepdims=True) + jnp.sum(
            prefix_weights, axis=1, keepdims=True
        )
        rounded = pltpu.roll(weights, heads, 1).astype(jnp.bfloat16)
        attended = [
            jnp.dot(
                rounded[i * row_heads : (i + 1) * row_heads],
                own_kv[i],
                preferred_element_type=jnp.float32,
            )
            for i in range(batch)
        ]
        wide = jnp.dot(
            prefix_weights.astype(jnp.bfloat16), values, preferred_element_type=jnp.float32
        )
        acc_ref[rows] = jnp.concatenate(attended, axis=0) + head_select(wide, heads, group)
        lane = lax.broadcasted_iota(jnp.int32, (block_rows, lanes), 1)
        stat_ref[rows] = jnp.where(lane < lanes // 2, row_max, total)
        return carry

    lax.fori_loop(0, q_ref.shape[0] // block_rows, one_block, 0)


def finish_body(sizes, shifts, *refs):
    heads, group, page, scale, block_rows, replicas = sizes
    table_ref, count_ref, q_ref, acc_ref, stat_ref = refs[:5]
    raws = refs[5 : 5 + len(shifts)]
    out_ref, keys_ref, values_ref = refs[5 + len(shifts) :]
    kinds = 2 * heads
    row_heads = heads * group
    me = lax.axis_index("replica")
    slots = raws[0].shape[0] // (page * kinds)
    fill_tables(raws, page_order(page * kinds, kinds), keys_ref, values_ref, heads, page)
    owners = [lax.rem(me + replicas - shift, replicas) for shift in shifts]
    live = live_lanes(
        table_ref, [owner * slots + s for owner in owners for s in range(slots)], page
    )
    live_rows = count_ref[0] * row_heads
    keys = keys_ref[...]
    values = values_ref[...]
    for start in range(0, q_ref.shape[0], block_rows):
        rows = pl.ds(start, block_rows)
        score = contract_last(head_concat(q_ref[rows], heads, group), keys) * scale
        score = jnp.where(live > 0, score, masked_score)
        stat = stat_ref[rows]
        earlier_max = stat[:, :1]
        row_max = jnp.maximum(earlier_max, jnp.max(score, axis=1, keepdims=True))
        weights = jnp.exp2(score - row_max)
        factor = jnp.exp2(earlier_max - row_max)
        total = stat[:, lanes // 2 : lanes // 2 + 1] * factor + jnp.sum(
            weights, axis=1, keepdims=True
        )
        wide = jnp.dot(weights.astype(jnp.bfloat16), values, preferred_element_type=jnp.float32)
        attended = acc_ref[rows] * factor + head_select(wide, heads, group)
        result = attended / total
        row = start + lax.broadcasted_iota(jnp.int32, result.shape, 0)
        out_ref[rows] = jnp.where(row < live_rows, result, 0.0).astype(jnp.bfloat16)


def vmem():
    return pl.BlockSpec(memory_space=pltpu.VMEM)


def smem():
    return pl.BlockSpec(memory_space=pltpu.SMEM)


def shards(replicas, queries, prefix_pool, page_table, suffix_kv, new_kv, suffix_len, counts):
    requests, head_count, width = queries.shape
    slots, page, unused, heads, width = prefix_pool.shape
    suffix = suffix_kv.shape[1]
    group = head_count // heads
    kinds = 2 * heads
    scale = width**-0.5 * math.log2(math.e)
    q = queries.reshape(requests * head_count, width)
    raw = prefix_pool.reshape(slots * page * kinds, width)
    batch = (-suffix * kinds) % lanes // kinds
    rows = requests * head_count
    others = [
        lax.ppermute(raw, "replica", [(i, (i + shift) % replicas) for i in range(replicas)])
        for shift in range(1, replicas)
    ]
    sizes = (heads, group, page, suffix, scale, batch)
    acc, stat = pl.pallas_call(
        functools.partial(local_body, sizes),
        out_shape=[jax.ShapeDtypeStruct((rows, width), jnp.float32)] * 2,
        in_specs=[smem(), smem(), vmem(), vmem(), vmem(), vmem()],
        out_specs=[vmem(), vmem()],
        scratch_shapes=[pltpu.VMEM((slots * page, heads * width), jnp.bfloat16)] * 2,
        compiler_params=pltpu.CompilerParams(vmem_limit_bytes=24 << 20),
        cost_estimate=pl.CostEstimate(
            flops=4 * rows * (slots * page + suffix) * width,
            bytes_accessed=6 << 20,
            transcendentals=rows * 256,
        ),
        name="local_part",
    )(
        page_table,
        suffix_len,
        q,
        raw,
        suffix_kv.reshape(requests * suffix * kinds, width),
        new_kv.reshape(requests * kinds, width),
    )
    tokens = (replicas - 1) * slots * page
    sizes = (heads, group, page, scale, 256, replicas)
    out = pl.pallas_call(
        functools.partial(finish_body, sizes, tuple(range(1, replicas))),
        out_shape=jax.ShapeDtypeStruct((rows, width), jnp.bfloat16),
        in_specs=[smem(), smem()] + [vmem()] * (3 + len(others)),
        out_specs=vmem(),
        scratch_shapes=[pltpu.VMEM((tokens, heads * width), jnp.bfloat16)] * 2,
        compiler_params=pltpu.CompilerParams(vmem_limit_bytes=24 << 20),
        cost_estimate=pl.CostEstimate(
            flops=4 * rows * tokens * width, bytes_accessed=3 << 20, transcendentals=rows * tokens
        ),
        name="finish_part",
    )(page_table, counts, q, acc, stat, *others)
    return out.reshape(requests, head_count, width)


def solution(mesh):
    placed = (
        P(("groups", "replica"), "tensor", None),
        P(("groups", "replica"), None, None, "tensor", None),
        P("groups"),
        P(("groups", "replica"), None, None, "tensor", None),
        P(("groups", "replica"), None, "tensor", None),
        P(("groups", "replica")),
        P(("groups", "replica")),
    )
    return jax.shard_map(
        functools.partial(shards, mesh.shape["replica"]),
        mesh=mesh,
        in_specs=placed,
        out_specs=P(("groups", "replica"), "tensor", None),
        check_vma=False,
    )
```

time: 32.4 us -> 21.6 us (0.67)
  blocking collectives: 17.4 us -> 0 us
  Pallas kernels: 0 us -> 9.22 us
  starting transfers between devices: 0 us -> 6.06 us
  matrix products: 5.68 us -> 0 us
  other arithmetic: 4.1 us -> 0 us
  local copies, waits for them, and re-layouts: 4.11 us -> 5.41 us
    all_gather x1 -> x0, blocking collectives: 17.4 us -> none  [prefix_rows(): lax.all_gather(prefix_pool, 'replica', axis=0, tiled=True)]
    pallas_call x0 -> x2, Pallas kernels: none -> 9.22 us  [the longest x1 5.85 us: shards(): pl.pallas_call(functools.partial(local_body, sizes), out_shape=[jax.Shape...]
    ppermute x0 -> x3, starting transfers between devices: none -> 6.06 us  [shards(): lax.ppermute(raw, 'replica', [(i, (i + shift) % replicas) for i in range(...]
    dot_general x5 -> x0, matrix products: 5.68 us -> none  [the longest x1 2.66 us: contract(): jnp.einsum('rgqk,kgd->rgqd', weights, block[:, 1], preferred_element_type...]
    unnamed x7 -> x14, local copies, waits for them, and re-layouts: 1.11 us -> 5.41 us
    reduce_sum x2 -> x0, other arithmetic: 1.67 us -> none  [absorb(): row_total = running[1] * factor + jnp.sum(weights, axis=-1)]
    slice x1 -> x0, local copies, waits for them, and re-layouts: 1.08 us -> none  [suffix_part(): suffix_kv[:, :, 0]]
    another operation x2 -> x0, other arithmetic: 0.84 us -> none
  transfers between devices with their start and end apart: 0 -> 3, of which waited for: 0 -> 0; matrix products, arithmetic and copies ran while one was open for 0% -> 0% of each run, Pallas kernels for 0% -> 27%
where the time goes in v1:
time: 21.6 us; the launch traced here: 21.4 us
  Pallas kernels  9.22 us (43%)
  starting transfers between devices  6.06 us (28%)
  local copies, waits for them, and re-layouts  5.41 us (25%)
  between operations  0.69 us (3%)
    ppermute x3, starting transfers between devices, shards(): lax.ppermute(raw, 'replica', [(i, (i + shift) % replicas) for i in range(...  6.06 us
    pallas_call x1, Pallas kernels, shards(): pl.pallas_call(functools.partial(local_body, sizes), out_shape=[jax.Shape...  5.85 us
    unnamed x14, local copies, waits for them, and re-layouts  5.41 us
    pallas_call x1, Pallas kernels, shards(): pl.pallas_call(functools.partial(finish_body, sizes, tuple(range(1, repli...  3.37 us
  transfers between devices with their start and end apart: 3, of which 0 were waited for; matrix products, arithmetic and copies ran while one was open for 0% of the time, Pallas kernels for 27%

profile of v1, /device:TPU:0, one launch (start us, length us, event | category | flops | bytes accessed | tf_op | source)
XLA Modules:
  0.0 21.4 jit_solution(633826206605085857)
XLA Ops:
  0.0 5.0 %collective-permute-start.2 = (bf16[512,128]{1,0:T(8,128)(2,1)}, bf16[512,128]{1,0:T(8,128)(2,1)S(1)}, u32[]{:S(2)}, u32[]{:S(2)}) collective-permute-start(bf16[512,128]{1,0:T(8,128)(2,1)} %bitcast.8), channel_id=1, source_target_pairs={{0,12},{4,0},{8,4},{12,8},{1,13},{5,1},{9,5},{13,9},{2,14},{6,2},{... | collective-permute-start | bytes 393224 | tf_op jit(solution)/shard_map/ppermute | solution.py:207
  5.0 0.0 collective-permute-start.1
  5.1 1.0 %collective-permute-start = (bf16[512,128]{1,0:T(8,128)(2,1)}, bf16[512,128]{1,0:T(8,128)(2,1)S(1)}, u32[]{:S(2)}, u32[]{:S(2)}) collective-permute-start(bf16[512,128]{1,0:T(8,128)(2,1)} %bitcast.10), channel_id=1, source_target_pairs={{0,4},{4,8},{8,12},{12,0},{1,5},{5,9},{9,13},{13,1},{2,6},{6,10},{... | collective-permute-start | bytes 393224 | tf_op jit(solution)/shard_map/ppermute | solution.py:207
  6.7 0.0 copy-start
  6.7 1.4 %copy-done = bf16[64,24,2,2,128]{4,3,2,1,0:T(2,128)(2,1)S(1)} copy-done((bf16[64,24,2,2,128]{4,3,2,1,0:T(2,128)(2,1)S(1)}, bf16[64,24,2,2,128]{4,3,2,1,0:T(2,128)(2,1)}, u32[]{:S(2)}) %copy-start) | copy-done | bytes 1572888
  8.1 0.0 copy-start.1
  8.1 0.9 %copy-done.1 = bf16[64,16,128]{2,1,0:T(8,128)(2,1)S(1)} copy-done((bf16[64,16,128]{2,1,0:T(8,128)(2,1)S(1)}, bf16[64,16,128]{2,1,0:T(8,128)(2,1)}, u32[]{:S(2)}) %copy-start.1) | copy-done | bytes 262168
  9.1 0.0 copy-start.3
  9.1 0.9 %copy-done.3 = bf16[2,64,2,2,128]{4,3,2,1,0:T(2,128)(2,1)S(1)} copy-done((bf16[2,64,2,2,128]{4,3,2,1,0:T(2,128)(2,1)S(1)}, bf16[2,64,2,2,128]{4,3,2,1,0:T(2,128)(2,1)}, u32[]{:S(2)}) %copy-start.3) | copy-done | bytes 131096
  10.0 0.0 copy-start.4
  10.0 0.8 %copy-done.4 = bf16[64,2,2,128]{3,2,1,0:T(2,128)(2,1)S(1)} copy-done((bf16[64,2,2,128]{3,2,1,0:T(2,128)(2,1)S(1)}, bf16[64,2,2,128]{3,2,1,0:T(2,128)(2,1)}, u32[]{:S(2)}) %copy-start.4) | copy-done | bytes 65560
  10.8 0.0 copy-start.5
  10.8 0.7 %copy-done.5 = s32[6]{0:T(128)S(1)} copy-done((s32[6]{0:T(128)S(1)}, s32[6]{0:T(128)}, u32[]{:S(2)}) %copy-start.5) | copy-done | bytes 48
  11.5 0.0 copy-start.6
  11.5 0.7 %copy-done.6 = s32[64]{0:T(128)S(1)} copy-done((s32[64]{0:T(128)S(1)}, s32[64]{0:T(128)}, u32[]{:S(2)}) %copy-start.6) | copy-done | bytes 280
  12.1 0.0 copy-start.2
  12.1 5.9 %local_part.1 = (f32[1024,128]{1,0:T(8,128)S(1)}, f32[1024,128]{1,0:T(8,128)S(1)}) custom-call(s32[6]{0:T(128)S(1)} %copy-done.5, s32[64]{0:T(128)S(1)} %copy-done.6, bf16[1024,128]{1,0:T(8,128)(2,1)S(1)} %bitcast.6, bf16[512,128]{1,0:T(8,128)(2,1)S(1)} %bitcast.11, bf16[6144,128]{1,0:T(8,128)(2,1)S(1)} %bitcast.5, bf16[256,128]{1,0:T(8,128)(2,1)S(1)} %bitcast.12), custom_call_target="tpu_custom_call" | custom-call | flops 79691776 | bytes 6291456 | tf_op jit(solution)/shard_map/local_part/pallas_call | solution.py:211
  18.0 0.0 collective-permute-done.2.refs_7_
  18.0 0.0 collective-permute-done.1.refs_6_
  18.0 0.0 collective-permute-done.refs_5_
  18.0 0.0 copy-done.2
  18.0 3.4 %finish_part.1 = bf16[1024,128]{1,0:T(8,128)(2,1)} custom-call(s32[6]{0:T(128)S(1)} %copy-done.5, s32[1]{0:T(128)S(6)} %copy.8.refs_1_, bf16[1024,128]{1,0:T(8,128)(2,1)S(1)} %bitcast.7, f32[1024,128]{1,0:T(8,128)S(1)} %get-tuple-element.7.refs_3_, f32[1024,128]{1,0:T(8,128)S(1)} %get-tuple-element.8.refs_4_, ...), custom_call_target="tpu_custom_call" | custom-call | flops 201326592 | bytes 3145728 | tf_op jit(solution)/shard_map/finish_part/pallas_call | solution.py:234
Async XLA Ops:
  0.0 18.0 %collective-permute-start.2 = (bf16[512,128]{1,0:T(8,128)(2,1)}, bf16[512,128]{1,0:T(8,128)(2,1)S(1)}, u32[]{:S(2)}, u32[]{:S(2)}) collective-permute-start(bf16[512,128]{1,0:T(8,128)(2,1)} %bitcast.8), channel_id=1, source_target_pairs={{0,12},{4,0},{8,4},{12,8},{1,13},{5,1},{9,5},{13,9},{2,14},{6,2},{... | collective-permute-start | bytes 393224 | tf_op jit(solution)/shard_map/ppermute | solution.py:207
  5.0 12.9 %collective-permute-start.1 = (bf16[512,128]{1,0:T(8,128)(2,1)}, bf16[512,128]{1,0:T(8,128)(2,1)S(1)}, u32[]{:S(2)}, u32[]{:S(2)}) collective-permute-start(bf16[512,128]{1,0:T(8,128)(2,1)} %bitcast.9), channel_id=1, source_target_pairs={{0,8},{4,12},{8,0},{12,4},{1,9},{5,13},{9,1},{13,5},{2,10},{6,14},... | collective-permute-start | bytes 393224 | tf_op jit(solution)/shard_map/ppermute | solution.py:207
  5.1 13.0 %collective-permute-start = (bf16[512,128]{1,0:T(8,128)(2,1)}, bf16[512,128]{1,0:T(8,128)(2,1)S(1)}, u32[]{:S(2)}, u32[]{:S(2)}) collective-permute-start(bf16[512,128]{1,0:T(8,128)(2,1)} %bitcast.10), channel_id=1, source_target_pairs={{0,4},{4,8},{8,12},{12,0},{1,5},{5,9},{9,13},{13,1},{2,6},{6,10},{... | collective-permute-start | bytes 393224 | tf_op jit(solution)/shard_map/ppermute | solution.py:207
  6.7 1.4 %copy-start = (bf16[64,24,2,2,128]{4,3,2,1,0:T(2,128)(2,1)S(1)}, bf16[64,24,2,2,128]{4,3,2,1,0:T(2,128)(2,1)}, u32[]{:S(2)}) copy-start(bf16[64,24,2,2,128]{4,3,2,1,0:T(2,128)(2,1)} %param.10) | copy-start | bytes 4718596
  8.1 0.9 %copy-start.1 = (bf16[64,16,128]{2,1,0:T(8,128)(2,1)S(1)}, bf16[64,16,128]{2,1,0:T(8,128)(2,1)}, u32[]{:S(2)}) copy-start(bf16[64,16,128]{2,1,0:T(8,128)(2,1)} %param.7) | copy-start | bytes 786436
  9.1 0.9 %copy-start.3 = (bf16[2,64,2,2,128]{4,3,2,1,0:T(2,128)(2,1)S(1)}, bf16[2,64,2,2,128]{4,3,2,1,0:T(2,128)(2,1)}, u32[]{:S(2)}) copy-start(bf16[2,64,2,2,128]{4,3,2,1,0:T(2,128)(2,1)} %param.8) | copy-start | bytes 393220
  10.0 0.8 %copy-start.4 = (bf16[64,2,2,128]{3,2,1,0:T(2,128)(2,1)S(1)}, bf16[64,2,2,128]{3,2,1,0:T(2,128)(2,1)}, u32[]{:S(2)}) copy-start(bf16[64,2,2,128]{3,2,1,0:T(2,128)(2,1)} %param.11) | copy-start | bytes 196612
  10.8 0.7 %copy-start.5 = (s32[6]{0:T(128)S(1)}, s32[6]{0:T(128)}, u32[]{:S(2)}) copy-start(s32[6]{0:T(128)} %refs_0_.1) | copy-start | bytes 76
  11.5 0.7 %copy-start.6 = (s32[64]{0:T(128)S(1)}, s32[64]{0:T(128)}, u32[]{:S(2)}) copy-start(s32[64]{0:T(128)} %lens_ref.1) | copy-start | bytes 772
  12.1 5.9 %copy-start.2 = (bf16[64,16,128]{2,1,0:T(8,128)(2,1)S(1)}, bf16[64,16,128]{2,1,0:T(8,128)(2,1)}, u32[]{:S(2)}) copy-start(bf16[64,16,128]{2,1,0:T(8,128)(2,1)} %param.7) | copy-start | bytes 786436
